TPU v7x, 256 devices: a whole 4x4x8 slice. The times are simulated.
256 devices in a mesh: dp: 64 (over x, z, core), mp: 4 (over y).
Axes of the slice: x: 4, y: 4, z: 8, core: 2. Of those that a mesh axis runs over, the one named last changes fastest.
Arguments:
- gradient: bfloat16 [64, 3, 192, 7168], P('dp', None, None, 'mp'), may hold values from -52 to 52
- error_memory: float32 [64, 3, 192, 7168], P('dp', None, None, 'mp'), may hold values from -4 to 4
- right_factor_initial: float32 [3, 32, 7168], P(None, None, 'mp'), may hold values from -6 to 6
Outputs:
- right_factor_next: float32 [3, 32, 7168], P(None, None, 'mp')
- error_next: float32 [64, 3, 192, 7168], P('dp', None, None, 'mp')
All inputs are finite; a program needn't handle non-finite values.
Results may differ from a plain program's by a relative error of at most 0.0003.
Values sent between devices are 32-bit elements; how exact they have to be, the bound alone decides.
A program may use at most 64 MiB of HBM per device.

v0:
```python
import jax
import jax.numpy as jnp
from jax import lax
from jax.sharding import PartitionSpec as P


def by_schmidt(left_factor_rows):

    def single(matrix_rows):
        item_count = matrix_rows.shape[0]

        def advance(column, column_basis):
            vector = lax.dynamic_index_in_dim(matrix_rows, column, 0, keepdims=False)
            coeffs = jnp.dot(column_basis, vector, precision=lax.Precision.HIGHEST)
            coeffs = jnp.where(jnp.arange(item_count) < column, coeffs, 0.0)
            vector = vector - jnp.dot(coeffs, column_basis, precision=lax.Precision.HIGHEST)
            vector = vector / jnp.sqrt(jnp.sum(vector * vector))
            return lax.dynamic_update_index_in_dim(column_basis, vector, column, 0)

        return lax.fori_loop(0, item_count, advance, jnp.zeros_like(matrix_rows))

    return jax.vmap(single)(left_factor_rows)


def orthonormal(left_factor_rows):
    return by_schmidt(left_factor_rows)


def per_device(gradient, error_memory, right_factor_initial):
    replicas = lax.axis_size("dp")
    corrected = gradient[0].astype(jnp.float32) + error_memory[0]
    basis_list = []
    q_list = []
    for bucket in range(corrected.shape[0]):
        bucket_matrix = corrected[bucket : bucket + 1]
        p_local = jnp.einsum(
            "bkc,brc->bkr",
            right_factor_initial[bucket : bucket + 1],
            bucket_matrix,
            precision=lax.Precision.HIGHEST,
        )
        left_factor_rows = lax.psum(p_local, ("dp", "mp")) / replicas
        bucket_basis = orthonormal(left_factor_rows)
        q_local = jnp.einsum(
            "bkr,brc->bkc", bucket_basis, bucket_matrix, precision=lax.Precision.HIGHEST
        )
        q_list.append(lax.psum(q_local, "dp") / replicas)
        basis_list.append(bucket_basis)
    column_basis = jnp.concatenate(basis_list, axis=0)
    right_factor_next = jnp.concatenate(q_list, axis=0)
    approximation = jnp.einsum(
        "bkr,bkc->brc", column_basis, right_factor_next, precision=lax.Precision.HIGHEST
    )
    error_next = corrected - approximation
    return (right_factor_next, error_next[None])


def solution(mesh):
    placed = (P("dp", None, None, "mp"), P("dp", None, None, "mp"), P(None, None, "mp"))
    return jax.shard_map(
        per_device,
        mesh=mesh,
        in_specs=placed,
        out_specs=(P(None, None, "mp"), P("dp", None, None, "mp")),
        check_vma=False,
    )
```

profile of v0, /device:TPU:1, one launch (start us, length us, event | category | flops | bytes accessed | tf_op | source)
XLA Modules:
  0.0 787.2 jit_solution(13062972051332310707)
XLA Ops:
  7.2 3.3 convert_add_fusion
  10.5 1.9 fusion.25
  12.5 1.9 fusion.26
  14.4 1.9 fusion.27
  16.4 246.1 %all-reduce.5.cloned.1.call-done = (f32[1,32,192]{2,1,0:T(8,128)}, f32[1,32,192]{2,1,0:T(8,128)}, f32[1,32,192]{2,1,0:T(8,128)}) async-done(((f32[1,32,192]{2,1,0:T(8,128)}, f32[1,32,192]{2,1,0:T(8,128)}, f32[1,32,192]{2,1,0:T(8,128)}), (f32[1,32,192]{2,1,0:T(8,128)}, f32[1,32,192]{2,1,0:T(8,128)}, f32[1,32,192]{2,1,0:T(8,128)})) %all-reduce.5.cloned.1.call-update) | async-done | bytes 73744 | tf_op jit(solution)/shard_map/psum | solution.py:42
  263.3 105.2 %while.47 = (s32[]{:T(128)}, f32[1,32,192]{2,1,0:T(8,128)S(1)}, f32[1,32,192]{2,1,0:T(8,128)S(1)}, s32[]{:T(128)}, s32[1]{0:T(128)}, /*index=5*/s32[3]{0:T(128)S(1)}, s32[2]{0:T(128)S(1)}, s32[]{:T(128)}) while((s32[]{:T(128)}, f32[1,32,192]{2,1,0:T(8,128)S(1)}, f32[1,32,192]{2,1,0:T(8,128)S(1)}, s32[]{:T(128)}, s32[1]{0:T(128)}, ...), condition=%wide.region_16.17_spmd, body=%wide.region_13.0_spmd.sunk | while | flops 148501 | bytes 60351 | solution.py:20
  368.5 105.2 %while.46 = (s32[]{:T(128)}, f32[1,32,192]{2,1,0:T(8,128)S(1)}, f32[1,32,192]{2,1,0:T(8,128)S(1)}, s32[]{:T(128)}, s32[1]{0:T(128)}, /*index=5*/s32[3]{0:T(128)S(1)}, s32[2]{0:T(128)S(1)}, s32[]{:T(128)}) while((s32[]{:T(128)}, f32[1,32,192]{2,1,0:T(8,128)S(1)}, f32[1,32,192]{2,1,0:T(8,128)S(1)}, s32[]{:T(128)}, s32[1]{0:T(128)}, ...), condition=%wide.region_10.11_spmd, body=%wide.region_7.10_spmd.sunk | while | flops 148501 | bytes 60351 | solution.py:20
  474.5 108.7 %while.45 = (s32[]{:T(128)}, f32[1,32,192]{2,1,0:T(8,128)S(1)}, f32[1,32,192]{2,1,0:T(8,128)S(1)}, s32[]{:T(128)}, s32[1]{0:T(128)}, /*index=5*/s32[3]{0:T(128)S(1)}, s32[2]{0:T(128)S(1)}, s32[]{:T(128)}) while((s32[]{:T(128)}, f32[1,32,192]{2,1,0:T(8,128)S(1)}, f32[1,32,192]{2,1,0:T(8,128)S(1)}, s32[]{:T(128)}, s32[1]{0:T(128)}, ...), condition=%wide.region_4.5_spmd, body=%wide.region_1.4_spmd.sunk | while | flops 148501 | bytes 60351 | solution.py:20
  474.6 0.8 and_reduce_fusion.6
  477.9 0.8 and_reduce_fusion.6
  481.3 0.8 and_reduce_fusion.6
  484.7 0.8 and_reduce_fusion.6
  488.1 0.8 and_reduce_fusion.6
  491.5 0.8 and_reduce_fusion.6
  494.9 0.8 and_reduce_fusion.6
  498.3 0.8 and_reduce_fusion.6
  501.7 0.8 and_reduce_fusion.6
  505.1 0.8 and_reduce_fusion.6
  508.5 0.8 and_reduce_fusion.6
  511.9 0.8 and_reduce_fusion.6
  515.3 0.8 and_reduce_fusion.6
  518.7 0.8 and_reduce_fusion.6
  522.1 0.8 and_reduce_fusion.6
  525.5 0.8 and_reduce_fusion.6
  528.9 0.8 and_reduce_fusion.6
  532.3 0.8 and_reduce_fusion.6
  535.7 0.8 and_reduce_fusion.6
  539.1 0.8 and_reduce_fusion.6
  542.5 0.8 and_reduce_fusion.6
  545.9 0.8 and_reduce_fusion.6
  549.3 0.8 and_reduce_fusion.6
  552.7 0.8 and_reduce_fusion.6
  556.1 0.8 and_reduce_fusion.6
  559.5 0.8 and_reduce_fusion.6
  562.9 0.8 and_reduce_fusion.6
  566.3 0.8 and_reduce_fusion.6
  569.7 0.8 and_reduce_fusion.6
  573.1 0.8 and_reduce_fusion.6
  576.5 0.8 and_reduce_fusion.6
  579.9 0.8 and_reduce_fusion.6
  583.2 3.0 convolution_bitcast_fusion.5
  586.1 2.9 convolution_bitcast_fusion.4
  589.1 2.9 convolution_bitcast_fusion.3
  592.0 178.5 %all-reduce.7.cloned.1.call-done = (f32[1,32,1792]{2,1,0:T(8,128)}, f32[1,32,1792]{2,1,0:T(8,128)}, f32[1,32,1792]{2,1,0:T(8,128)}) async-done(((f32[1,32,1792]{2,1,0:T(8,128)}, f32[1,32,1792]{2,1,0:T(8,128)}, f32[1,32,1792]{2,1,0:T(8,128)}), (f32[1,32,1792]{2,1,0:T(8,128)}, f32[1,32,1792]{2,1,0:T(8,128)}, f32[1,32,1792]{2,1,0:T(8,128)})) %all-reduce.7.cloned.1.call-update) | async-done | bytes 688144 | tf_op jit(solution)/shard_map/psum | solution.py:47
  770.6 1.0 broadcast_multiply_fusion
  771.5 1.0 broadcast_multiply_fusion.1
  772.5 1.0 broadcast_multiply_fusion.2
  773.5 6.8 fusion.21
  (948 shorter events, 224.7 us)
Async XLA Ops:
  7.2 3.3 copy-start.2
  7.2 255.3 %all-reduce.5.cloned.1.call-start = ((), (), s32[]{:S(2)}) async-start(), calls=%async_computation | async-start | bytes 196608 | tf_op jit(solution)/shard_map/psum | solution.py:42
  10.5 3.9 copy-start
  10.5 252.7 %copy-start.3 = (s32[2]{0:T(128)S(1)}, s32[2]{0:T(128)}, u32[]{:S(2)}) copy-start(s32[2]{0:T(128)} %constant.252.clone.1) | copy-start | bytes 28
  10.5 252.7 %copy-start.4 = (s32[3]{0:T(128)S(1)}, s32[3]{0:T(128)}, u32[]{:S(2)}) copy-start(s32[3]{0:T(128)} %constant.253.clone.1) | copy-start | bytes 40
  16.3 754.3 %all-reduce.7.cloned.1.call-start = ((), (), s32[]{:S(2)}) async-start(), calls=%async_computation.1 | async-start | bytes 1376256 | tf_op jit(solution)/shard_map/psum | solution.py:47
  773.5 6.8 copy-start.1
Sparse Core Ops, SparseCore 0:
  16.5 245.9 all-reduce.4
  592.2 178.3 all-reduce.6
where the time goes:
time: 790 us; the launch traced here: 787 us
  waiting for transfers between devices  425 us (54%)
  other arithmetic  218 us (28%)
  loops' own time  70.9 us (9%)
  matrix products  47.6 us (6%)
  between operations  14.2 us (2%)
  local copies, waits for them, and re-layouts  11.5 us (1%)
    psum x1, waiting for transfers between devices, per_device(): left_factor_rows = lax.psum(p_local, ('dp', 'mp')) / replicas  246 us
    psum x1, waiting for transfers between devices, per_device(): q_list.append(lax.psum(q_local, 'dp') / replicas)  179 us
    another operation x192, other arithmetic  136 us
    another operation x3, loops' own time, single(): return lax.fori_loop(0, item_count, advance, jnp.zeros_like(matrix_rows))  70.9 us
    reduce_sum x96, other arithmetic, advance(): vector = vector / jnp.sqrt(jnp.sum(vector * vector))  59.6 us
  transfers between devices with their start and end apart: 2, of which 2 were waited for; matrix products, arithmetic and copies ran while one was open for 0% of the time, Pallas kernels for 0%

commit v1 on v0

v1 whole, which is shorter than its diff:
```python
import functools

import jax
import jax.numpy as jnp
from jax import lax
from jax.experimental import pallas as pl
from jax.experimental.pallas import tpu as pltpu
from jax.sharding import PartitionSpec as P

MESH = pl.DeviceIdType.MESH
NX, NY, NZ = 4, 4, 8
BUCKETS, RANK, ROWS = 3, 32, 192
GROUP = NX * NY
PIECE = ROWS // GROUP
XY = [(i, j) for i in range(NX) for j in range(NY) if i or j]
F32, BF16 = jnp.float32, jnp.bfloat16
HIGHEST = lax.Precision.HIGHEST


def place():
    dp = lax.axis_index("dp")
    return dp // (2 * NZ), lax.axis_index("mp"), (dp // 2) % NZ, dp % 2


def device(x, y, z, c):
    return ((x * NZ + z) * 2 + c, y)


def split(value):
    high = value.astype(BF16)
    return high, (value - high.astype(F32)).astype(BF16)


def dot(a, b, dims=((1,), (0,))):
    return lax.dot_general(a, b, (dims, ((), ())), preferred_element_type=F32)


def inverse_factor(gram, lane):
    column = lane % RANK
    row = lax.broadcasted_iota(jnp.int32, (RANK, 128), 0)
    group = lane - column
    z = gram
    done = jnp.zeros((RANK, 128), F32)
    block = 8
    for start in range(0, RANK, block):
        cols = [
            jnp.take_along_axis(z, group + (start + t), axis=1) for t in range(block)
        ]
        for t in range(block):
            k = start + t
            scale = lax.rsqrt(cols[t][k : k + 1, :])
            below = jnp.where(row > k, cols[t] * scale, 0.0)
            pivot = jnp.where(column[k : k + 1] == k, scale, z[k : k + 1, :] * scale)
            done = jnp.where(row == k, pivot, done)
            z = jnp.where(column == k, 0.0, z) - below * pivot
            for u in range(t + 1, block):
                cols[u] = cols[u] - below * (cols[u][k : k + 1, :] * scale)
    return jnp.where(column <= row, done, 0.0)


def reduce_kernel(
    g_hbm, e_hbm, r_hbm, q_hbm, w_ref,
    g_ref, e_ref, r_ref, ch_ref, cl_ref, rr_ref,
    ps, pr, pcs, pcr, pzs, pzr, pg, pf,
    qs, qc, xs, xr, zs, zr, zg, qg,
    in_sem, out_sem,
    pa_s, pa_r, pc_s, pc_r, pz_s, pz_r, pg_s, pg_r,
    s1_s, s1_r, s2_s, s2_r, s3_s, s3_r, s4_s, s4_r, s5_s, s5_r, s6_s, s6_r,
):
    x, y, z, c = place()
    xy_peers = [((x + i) % NX, (y + j) % NY) for i, j in XY]
    x_peers = [(x + i) % NX for i in range(1, NX)]
    z_peers = [(z + i) % NZ for i in range(1, NZ)]
    mine = x * NY + y

    barrier = pltpu.get_barrier_semaphore()
    for px, py in xy_peers:
        pl.semaphore_signal(barrier, inc=1, device_id=device(px, py, z, c), device_id_type=MESH)
    for pz in z_peers:
        pl.semaphore_signal(barrier, inc=1, device_id=device(x, y, pz, c), device_id_type=MESH)
    pl.semaphore_signal(barrier, inc=1, device_id=device(x, y, z, 1 - c), device_id_type=MESH)

    loads = [pltpu.make_async_copy(r_hbm, r_ref, in_sem.at[0])]
    for b in range(BUCKETS):
        loads.append(pltpu.make_async_copy(g_hbm.at[0, b], g_ref.at[b], in_sem.at[1 + 2 * b]))
        loads.append(pltpu.make_async_copy(e_hbm.at[0, b], e_ref.at[b], in_sem.at[2 + 2 * b]))
    for load in loads:
        load.start()

    sends = []

    def send(src, dst, send_sem, recv_sem, where):
        copy = pltpu.make_async_remote_copy(
            src_ref=src, dst_ref=dst, send_sem=send_sem, recv_sem=recv_sem,
            device_id=device(*where), device_id_type=MESH,
        )
        copy.start()
        sends.append(copy)
        return copy

    width = r_ref.shape[2]
    loads[0].wait()
    rr_ref[...] = jnp.zeros_like(rr_ref)
    for b in range(BUCKETS):
        high, low = split(r_ref[b])
        rr_ref[b * RANK : (b + 1) * RANK, :] = high
        rr_ref[128 + b * RANK : 128 + (b + 1) * RANK, :] = low

    lane = lax.broadcasted_iota(jnp.int32, (RANK, 128), 1)
    lane_rows = lax.broadcasted_iota(jnp.int32, (ROWS, 128), 1)
    step = 16
    total = jnp.zeros((ROWS, 128), F32)
    for b in range(BUCKETS):
        loads[1 + 2 * b].wait()
        loads[2 + 2 * b].wait()

        @pl.loop(0, ROWS // step)
        def _(i):
            rows = pl.ds(pl.multiple_of(i * step, step), step)
            high, low = split(g_ref[b, rows, :].astype(F32) + e_ref[b, rows, :])
            ch_ref[b, rows, :] = high
            cl_ref[b, rows, :] = low

        both = dot(ch_ref[b], rr_ref[...], ((1,), (1,)))
        part = both[:, :128] + both[:, 128:] + dot(cl_ref[b], rr_ref[:128, :], ((1,), (1,)))
        total = jnp.where(lane_rows // RANK == b, part, total)
    total = total * (1.0 / 64)
    for i in range(GROUP):
        ps[i] = total[i * PIECE : (i + 1) * PIECE, :]

    pl.semaphore_wait(barrier, len(XY) + NZ)

    copies = [
        send(ps.at[px * NY + py], pr.at[i], pa_s.at[i], pa_r.at[i], (px, py, z, c))
        for i, (px, py) in enumerate(xy_peers)
    ]
    piece = ps[mine]
    for i, copy in enumerate(copies):
        copy.wait_recv()
        piece = piece + pr[i]
    pcs[...] = piece
    copy = send(pcs, pcr, pc_s, pc_r, (x, y, z, 1 - c))
    copy.wait_recv()
    piece = piece + pcr[...]
    pzs[...] = piece
    copies = [
        send(pzs, pzr.at[i], pz_s.at[i], pz_r.at[i], (x, y, pz, c)) for i, pz in enumerate(z_peers)
    ]
    for i, copy in enumerate(copies):
        copy.wait_recv()
        piece = piece + pzr[i]
    pg[mine] = piece
    copies = [
        send(pg.at[mine], pg.at[mine], pg_s.at[i], pg_r.at[i], (px, py, z, c))
        for i, (px, py) in enumerate(xy_peers)
    ]
    for copy in copies:
        copy.wait_recv()
    for i in range(GROUP):
        pf[i * PIECE : (i + 1) * PIECE, :] = pg[i]
    pf[ROWS:, :] = jnp.zeros((256 - ROWS, 128), F32)

    left_t = pf[...]
    left = left_t.T
    gram = lax.dot_general(
        left, left_t, (((1,), (0,)), ((), ())), precision=HIGHEST, preferred_element_type=F32
    )
    packed = jnp.zeros((RANK, 128), F32)
    for b in range(BUCKETS):
        packed = jnp.where(lane // RANK == b, gram[b * RANK : (b + 1) * RANK, :], packed)
    inverse = inverse_factor(packed, lane)
    blocks = [jnp.where(lane // RANK == b, inverse, 0.0) for b in range(BUCKETS)]
    blocks.append(jnp.zeros((RANK, 128), F32))
    basis = lax.dot_general(
        jnp.concatenate(blocks, axis=0), left, (((1,), (0,)), ((), ())),
        precision=HIGHEST, preferred_element_type=F32,
    )[:, :ROWS]
    basis_high, basis_low = split(basis)

    def local_q(b):
        rows = slice(b * RANK, (b + 1) * RANK)
        stacked = jnp.concatenate([basis_high[rows], basis_low[rows]], axis=0)
        half = width // 2
        for start in range(0, width, 256):
            stop = start + 256
            one = dot(stacked, ch_ref[b, :, start:stop])
            value = one[:RANK] + one[RANK:] + dot(basis_high[rows], cl_ref[b, :, start:stop])
            if stop <= half:
                qs[b, 0, :, start:stop] = value
            elif start >= half:
                qs[b, 1, :, start - half : stop - half] = value
            else:
                qs[b, 0, :, start:half] = value[:, : half - start]
                qs[b, 1, :, : stop - half] = value[:, half - start :]

    first, second, third, fourth, fifth, sixth = ({} for _ in range(6))
    tiles = width // 2 // 128

    def send_core(b):
        first[b] = send(qs.at[b, 1 - c], qc.at[b], s1_s.at[b], s1_r.at[b], (x, y, z, 1 - c))

    def send_x(b):
        first[b].wait_recv()
        for t in range(4):
            xs[b, t] = qs[b, c, 8 * t : 8 * t + 8, :] + qc[b, 8 * t : 8 * t + 8, :]
        second[b] = [
            send(xs.at[b, px], xr.at[b, i], s2_s.at[b, i], s2_r.at[b, i], (px, y, z, c))
            for i, px in enumerate(x_peers)
        ]

    def send_z(b):
        value = xs[b, x]
        for i, copy in enumerate(second[b]):
            copy.wait_recv()
            value = value + xr[b, i]
        for t in range(tiles):
            zs[b, t] = value[:, t * 128 : (t + 1) * 128]
        zs[b, tiles] = jnp.zeros((8, 128), F32)
        third[b] = [
            send(zs.at[b, pz], zr.at[b, i], s3_s.at[b, i], s3_r.at[b, i], (x, y, pz, c))
            for i, pz in enumerate(z_peers)
        ]

    def back_z(b):
        value = zs[b, z]
        for i, copy in enumerate(third[b]):
            copy.wait_recv()
            value = value + zr[b, i]
        zg[b, z] = value * (1.0 / 64)
        fourth[b] = [
            send(zg.at[b, z], zg.at[b, z], s4_s.at[b, i], s4_r.at[b, i], (x, y, pz, c))
            for i, pz in enumerate(z_peers)
        ]

    def back_x(b):
        for copy in fourth[b]:
            copy.wait_recv()
        for t in range(tiles):
            qg[b, c, x, :, t * 128 : (t + 1) * 128] = zg[b, t]
        fifth[b] = [
            send(qg.at[b, c, x], qg.at[b, c, x], s5_s.at[b, i], s5_r.at[b, i], (px, y, z, c))
            for i, px in enumerate(x_peers)
        ]

    def back_core(b):
        for copy in fifth[b]:
            copy.wait_recv()
        sixth[b] = send(qg.at[b, c], qg.at[b, c], s6_s.at[b], s6_r.at[b], (x, y, z, 1 - c))

    local_q(0)
    send_core(0)
    local_q(1)
    send_x(0)
    send_core(1)
    local_q(2)
    send_x(1)
    send_core(2)
    send_x(2)
    for b in range(BUCKETS):
        turned = basis[b * RANK : (b + 1) * RANK].T
        high, low = split(turned)
        w_ref[b] = jnp.concatenate([high, low, high, jnp.zeros((ROWS, RANK), BF16)], axis=1)
    for stage in (send_z, back_z, back_x, back_core):
        for b in range(BUCKETS):
            stage(b)
    outs = []
    for b in range(BUCKETS):
        sixth[b].wait_recv()
        out = pltpu.make_async_copy(qg.at[b], q_hbm.at[b], out_sem.at[b])
        out.start()
        outs.append(out)
    for copy in sends:
        copy.wait_send()
    for out in outs:
        out.wait()


def error_kernel(g_ref, e_ref, w_ref, q_ref, q_out, err_ref):
    half = q_ref.shape[-1]
    for h in range(2):
        q = jnp.concatenate([q_ref[0, h, t] for t in range(4)], axis=0)
        cols = slice(h * half, (h + 1) * half)
        q_out[0, :, cols] = q
        high, low = split(q)
        stacked = jnp.concatenate([high, high, low, jnp.zeros_like(high)], axis=0)
        approx = dot(w_ref[0], stacked)
        err_ref[0, 0, :, cols] = g_ref[0, 0, :, cols].astype(F32) + e_ref[0, 0, :, cols] - approx


def per_device(gradient, error_memory, right_factor_initial):
    width = right_factor_initial.shape[2]
    half = width // 2
    dma = pltpu.SemaphoreType.DMA
    vmem = pltpu.VMEM
    hbm = pl.BlockSpec(memory_space=pl.ANY)
    b3 = BUCKETS
    n_xy, n_x, n_z = len(XY), NX - 1, NZ - 1
    q, w = pl.pallas_call(
        reduce_kernel,
        out_shape=(
            jax.ShapeDtypeStruct((b3, 2, 4, 8, half), F32),
            jax.ShapeDtypeStruct((b3, ROWS, 128), BF16),
        ),
        in_specs=[hbm, hbm, hbm],
        out_specs=(hbm, pl.BlockSpec(memory_space=pltpu.VMEM)),
        scratch_shapes=[
            vmem((b3, ROWS, width), BF16),
            vmem((b3, ROWS, width), F32),
            vmem((b3, RANK, width), F32),
            vmem((b3, ROWS, width), BF16),
            vmem((b3, ROWS, width), BF16),
            vmem((256, width), BF16),
            vmem((GROUP, PIECE, 128), F32),
            vmem((n_xy, PIECE, 128), F32),
            vmem((PIECE, 128), F32),
            vmem((PIECE, 128), F32),
            vmem((PIECE, 128), F32),
            vmem((n_z, PIECE, 128), F32),
            vmem((GROUP, PIECE, 128), F32),
            vmem((256, 128), F32),
            vmem((b3, 2, RANK, half), F32),
            vmem((b3, RANK, half), F32),
            vmem((b3, 4, 8, half), F32),
            vmem((b3, n_x, 8, half), F32),
            vmem((b3, NZ, 8, 128), F32),
            vmem((b3, n_z, 8, 128), F32),
            vmem((b3, NZ, 8, 128), F32),
            vmem((b3, 2, 4, 8, half), F32),
            dma((1 + 2 * b3,)),
            dma((b3,)),
            dma((n_xy,)), dma((n_xy,)),
            dma, dma,
            dma((n_z,)), dma((n_z,)),
            dma((n_xy,)), dma((n_xy,)),
            dma((b3,)), dma((b3,)),
            dma((b3, n_x)), dma((b3, n_x)),
            dma((b3, n_z)), dma((b3, n_z)),
            dma((b3, n_z)), dma((b3, n_z)),
            dma((b3, n_x)), dma((b3, n_x)),
            dma((b3,)), dma((b3,)),
        ],
        compiler_params=pltpu.CompilerParams(
            collective_id=0, has_side_effects=True, vmem_limit_bytes=32 << 20
        ),
        name="reduce_kernel",
    )(gradient, error_memory, right_factor_initial)

    return pl.pallas_call(
        error_kernel,
        grid=(b3,),
        out_shape=(
            jax.ShapeDtypeStruct((b3, RANK, width), F32),
            jax.ShapeDtypeStruct((1, b3, ROWS, width), F32),
        ),
        in_specs=[
            pl.BlockSpec((1, 1, ROWS, width), lambda b: (0, b, 0, 0)),
            pl.BlockSpec((1, 1, ROWS, width), lambda b: (0, b, 0, 0)),
            pl.BlockSpec((1, ROWS, 128), lambda b: (b, 0, 0)),
            pl.BlockSpec((1, 2, 4, 8, half), lambda b: (b, 0, 0, 0, 0)),
        ],
        out_specs=(
            pl.BlockSpec((1, RANK, width), lambda b: (b, 0, 0)),
            pl.BlockSpec((1, 1, ROWS, width), lambda b: (0, b, 0, 0)),
        ),
        compiler_params=pltpu.CompilerParams(vmem_limit_bytes=32 << 20),
        name="error_kernel",
    )(gradient, error_memory, w, q)


def solution(mesh):
    placed = (P("dp", None, None, "mp"), P("dp", None, None, "mp"), P(None, None, "mp"))
    return jax.shard_map(
        per_device,
        mesh=mesh,
        in_specs=placed,
        out_specs=(P(None, None, "mp"), P("dp", None, None, "mp")),
        check_vma=False,
    )
```

time: 790 us -> 61.8 us (0.08)
  waiting for transfers between devices: 425 us -> 0 us
  other arithmetic: 218 us -> 0 us
  loops' own time: 70.9 us -> 0 us
  Pallas kernels: 0 us -> 56.1 us
  matrix products: 47.6 us -> 0 us
  between operations: 14.2 us -> 0.65 us
    psum x2 -> x0, waiting for transfers between devices: 425 us -> none  [the longest x1 246 us: per_device(): left_factor_rows = lax.psum(p_local, ('dp', 'mp')) / replicas]
    another operation x192 -> x0, other arithmetic: 136 us -> none
    another operation x3 -> x0, loops' own time: 70.9 us -> none  [single(): return lax.fori_loop(0, item_count, advance, jnp.zeros_like(matrix_rows))]
    reduce_sum x96 -> x0, other arithmetic: 59.6 us -> none  [advance(): vector = vector / jnp.sqrt(jnp.sum(vector * vector))]
    pallas_call x0 -> x2, Pallas kernels: none -> 56.1 us  [the longest x1 53.3 us: per_device(): pl.pallas_call(reduce_kernel, out_shape=(jax.ShapeDtypeStruct((b3, 2, 4,...]
    dot_general x199 -> x0, matrix products: 47.6 us -> none  [the longest x96 13.7 us: advance(): jnp.dot(coeffs, column_basis, precision=lax.Precision.HIGHEST)]
  transfers between devices with their start and end apart: 2 -> 0, of which waited for: 2 -> 0; matrix products, arithmetic and copies ran while one was open for 0% -> 0% of each run, Pallas kernels for 0% -> 0%
where the time goes in v1:
time: 61.8 us; the launch traced here: 61.6 us
  Pallas kernels  56.1 us (91%)
  local copies, waits for them, and re-layouts  4.84 us (8%)
  between operations  0.65 us (1%)
    pallas_call x1, Pallas kernels, per_device(): pl.pallas_call(reduce_kernel, out_shape=(jax.ShapeDtypeStruct((b3, 2, 4,...  53.3 us
    unnamed x6, local copies, waits for them, and re-layouts  4.84 us
    pallas_call x1, Pallas kernels, per_device(): pl.pallas_call(error_kernel, grid=(b3,), out_shape=(jax.ShapeDtypeStruct(...  2.84 us

profile of v1, /device:TPU:1, one launch (start us, length us, event | category | flops | bytes accessed | tf_op | source)
XLA Modules:
  0.0 61.6 jit_solution(5678794191613653636)
XLA Ops:
  0.6 0.0 copy-start
  0.6 2.2 %copy-done = f32[1,3,192,1792]{3,2,1,0:T(8,128)S(1)} copy-done((f32[1,3,192,1792]{3,2,1,0:T(8,128)S(1)}, f32[1,3,192,1792]{3,2,1,0:T(8,128)}, u32[]{:S(2)}) %copy-start) | copy-done | bytes 4128792
  2.8 0.0 copy-start.1
  2.8 1.6 %copy-done.1 = bf16[1,3,192,1792]{3,2,1,0:T(8,128)(2,1)S(1)} copy-done((bf16[1,3,192,1792]{3,2,1,0:T(8,128)(2,1)S(1)}, bf16[1,3,192,1792]{3,2,1,0:T(8,128)(2,1)}, u32[]{:S(2)}) %copy-start.1) | copy-done | bytes 2064408
  4.4 0.0 copy-start.2
  4.4 1.1 %copy-done.2 = f32[3,32,1792]{2,1,0:T(8,128)S(1)} copy-done((f32[3,32,1792]{2,1,0:T(8,128)S(1)}, f32[3,32,1792]{2,1,0:T(8,128)}, u32[]{:S(2)}) %copy-start.2) | copy-done | bytes 688152
  5.5 53.3 %reduce_kernel.1 = (f32[3,2,4,8,896]{4,3,2,1,0:T(8,128)S(1)}, bf16[3,192,128]{2,1,0:T(8,128)(2,1)S(1)}) custom-call(bf16[1,3,192,1792]{3,2,1,0:T(8,128)(2,1)S(1)} %copy-done.1, f32[1,3,192,1792]{3,2,1,0:T(8,128)S(1)} %copy-done, f32[3,32,1792]{2,1,0:T(8,128)S(1)} %copy-done.2), custom_call_target="tpu_custom_call" | custom-call | tf_op jit(solution)/shard_map/reduce_kernel/pallas_call | solution.py:298
  58.8 2.8 %error_kernel.1 = (f32[3,32,1792]{2,1,0:T(8,128)}, f32[1,3,192,1792]{3,2,1,0:T(8,128)}) custom-call(bf16[1,3,192,1792]{3,2,1,0:T(8,128)(2,1)S(1)} %copy-done.1, f32[1,3,192,1792]{3,2,1,0:T(8,128)S(1)} %copy-done, bf16[3,192,128]{2,1,0:T(8,128)(2,1)S(1)} %get-tuple-element.4.w_ref, f32[3,2,4,8,896]{4,3,2,1,0:T(8,128)S(1)} %get-tuple-element.5.q_ref), custom_call_target="tpu_custom_call" | custom-call | tf_op jit(solution)/shard_map/error_kernel/pallas_call | solution.py:348
Async XLA Ops:
  0.6 2.2 %copy-start = (f32[1,3,192,1792]{3,2,1,0:T(8,128)S(1)}, f32[1,3,192,1792]{3,2,1,0:T(8,128)}, u32[]{:S(2)}) copy-start(f32[1,3,192,1792]{3,2,1,0:T(8,128)} %e_ref.1) | copy-start | bytes 12386308
  2.8 1.6 %copy-start.1 = (bf16[1,3,192,1792]{3,2,1,0:T(8,128)(2,1)S(1)}, bf16[1,3,192,1792]{3,2,1,0:T(8,128)(2,1)}, u32[]{:S(2)}) copy-start(bf16[1,3,192,1792]{3,2,1,0:T(8,128)(2,1)} %g_ref.1) | copy-start | bytes 6193156
  4.4 1.1 %copy-start.2 = (f32[3,32,1792]{2,1,0:T(8,128)S(1)}, f32[3,32,1792]{2,1,0:T(8,128)}, u32[]{:S(2)}) copy-start(f32[3,32,1792]{2,1,0:T(8,128)} %r_hbm.1) | copy-start | bytes 2064388

commit v2 on v1

v2 whole, which is shorter than its diff:
```python
import functools

import jax
import jax.numpy as jnp
from jax import lax
from jax.experimental import pallas as pl
from jax.experimental.pallas import tpu as pltpu
from jax.sharding import PartitionSpec as P

MESH = pl.DeviceIdType.MESH
NX, NY, NZ = 4, 4, 8
BUCKETS, RANK, ROWS = 3, 32, 192
GROUP = NX * NY
PIECE = ROWS // GROUP
HOPS = [0, 1, 2, 1]
XY = sorted(
    ((i, j) for i in range(NX) for j in range(NY) if i or j), key=lambda p: -HOPS[p[0]] - HOPS[p[1]]
)
XS = [2, 1, 3]
ZS = [4, 3, 5, 2, 6, 1, 7]
F32, BF16 = jnp.float32, jnp.bfloat16
HIGHEST = lax.Precision.HIGHEST


def place():
    dp = lax.axis_index("dp")
    return dp // (2 * NZ), lax.axis_index("mp"), (dp // 2) % NZ, dp % 2


def device(x, y, z, c):
    return ((x * NZ + z) * 2 + c, y)


def split(value):
    high = value.astype(BF16)
    return high, (value - high.astype(F32)).astype(BF16)


def dot(a, b, dims=((1,), (0,))):
    return lax.dot_general(a, b, (dims, ((), ())), preferred_element_type=F32)


def eliminate(z, done, lane, start, stop):
    column = lane % RANK
    row = lax.broadcasted_iota(jnp.int32, (RANK, 128), 0)
    group = lane - column
    cols = [jnp.take_along_axis(z, group + k, axis=1) for k in range(start, stop)]
    for t in range(stop - start):
        k = start + t
        scale = lax.rsqrt(cols[t][k : k + 1, :])
        below = jnp.where(row > k, cols[t] * scale, 0.0)
        pivot = jnp.where(column[k : k + 1] == k, scale, z[k : k + 1, :] * scale)
        done = jnp.where(row == k, pivot, done)
        z = jnp.where(column == k, 0.0, z) - below * pivot
        for u in range(t + 1, stop - start):
            cols[u] = cols[u] - below * (cols[u][k : k + 1, :] * scale)
    return z, done


def reduce_kernel(
    c_ref, r_ref, q_ref, err_ref,
    ch_ref, cl_ref, rr_ref, w_ref,
    ps, pr, pcs, pcr, zp, pg, pf,
    qs, qc, xs, xr, zs, zr, zg, qg,
    pa_s, pa_r, pc_s, pc_r, pz_s, pz_r, pg_s, pg_r,
    s1_s, s1_r, s2_s, s2_r, s3_s, s3_r, s4_s, s4_r, s5_s, s5_r, s6_s, s6_r,
):
    x, y, z, c = place()
    xy_peers = [((x + i) % NX, (y + j) % NY) for i, j in XY]
    x_peers = [(x + i) % NX for i in XS]
    z_peers = [(z + i) % NZ for i in ZS]
    mine = x * NY + y

    barrier = pltpu.get_barrier_semaphore()
    for px, py in xy_peers:
        pl.semaphore_signal(barrier, inc=1, device_id=device(px, py, z, c), device_id_type=MESH)
    for pz in z_peers:
        pl.semaphore_signal(barrier, inc=1, device_id=device(x, y, pz, c), device_id_type=MESH)
    pl.semaphore_signal(barrier, inc=1, device_id=device(x, y, z, 1 - c), device_id_type=MESH)

    sends = []

    def send(src, dst, send_sem, recv_sem, where):
        copy = pltpu.make_async_remote_copy(
            src_ref=src, dst_ref=dst, send_sem=send_sem, recv_sem=recv_sem,
            device_id=device(*where), device_id_type=MESH,
        )
        copy.start()
        sends.append(copy)
        return copy

    width = r_ref.shape[2]
    rr_ref[...] = jnp.zeros_like(rr_ref)
    for b in range(BUCKETS):
        high, low = split(r_ref[b])
        rr_ref[b * RANK : (b + 1) * RANK, :] = high
        rr_ref[128 + b * RANK : 128 + (b + 1) * RANK, :] = low

    lane = lax.broadcasted_iota(jnp.int32, (RANK, 128), 1)
    lane_rows = lax.broadcasted_iota(jnp.int32, (ROWS, 128), 1)
    step = 256
    total = jnp.zeros((ROWS, 128), F32)
    for b in range(BUCKETS):
        both = jnp.zeros((ROWS, 256), F32)
        rest = jnp.zeros((ROWS, 128), F32)
        for start in range(0, width, step):
            cols = slice(start, start + step)
            value = c_ref[b, :, cols]
            high, low = split(value)
            ch_ref[b, :, cols] = high
            cl_ref[b, :, cols] = low
            both = both + dot(high, rr_ref[:, cols], ((1,), (1,)))
            rest = rest + dot(low, rr_ref[:128, cols], ((1,), (1,)))
        part = both[:, :128] + both[:, 128:] + rest
        total = jnp.where(lane_rows // RANK == b, part, total)
    total = total * (1.0 / 64)
    for i in range(GROUP):
        ps[i] = total[i * PIECE : (i + 1) * PIECE, :]

    pl.semaphore_wait(barrier, len(XY) + NZ)

    copies = [
        send(ps.at[px * NY + py], pr.at[i], pa_s.at[i], pa_r.at[i], (px, py, z, c))
        for i, (px, py) in enumerate(xy_peers)
    ]
    piece = ps[mine]
    for i, copy in enumerate(copies):
        copy.wait_recv()
        piece = piece + pr[i]
    pcs[...] = piece
    copy = send(pcs, pcr, pc_s, pc_r, (x, y, z, 1 - c))
    copy.wait_recv()
    piece = piece + pcr[...]
    zp[z] = piece
    copies = [
        send(zp.at[z], zp.at[z], pz_s.at[i], pz_r.at[i], (x, y, at, c)) for i, at in enumerate(z_peers)
    ]
    for copy in copies:
        copy.wait_recv()
    piece = zp[0]
    for i in range(1, NZ):
        piece = piece + zp[i]
    pg[mine] = piece
    copies = [
        send(pg.at[mine], pg.at[mine], pg_s.at[i], pg_r.at[i], (px, py, z, c))
        for i, (px, py) in enumerate(xy_peers)
    ]
    for copy in copies:
        copy.wait_recv()
    for i in range(GROUP):
        pf[i * PIECE : (i + 1) * PIECE, :] = pg[i]
    pf[ROWS:, :] = jnp.zeros((256 - ROWS, 128), F32)

    left_t = pf[...]
    left = left_t.T
    left_high, left_low = split(left[:, :ROWS])

    def local_t(b):
        rows = slice(b * RANK, (b + 1) * RANK)
        stacked = jnp.concatenate([left_high[rows], left_low[rows]], axis=0)
        half = width // 2
        for start in range(0, width, 256):
            stop = start + 256
            one = dot(stacked, ch_ref[b, :, start:stop])
            value = one[:RANK] + one[RANK:] + dot(left_high[rows], cl_ref[b, :, start:stop])
            if stop <= half:
                qs[b, 0, :, start:stop] = value
            elif start >= half:
                qs[b, 1, :, start - half : stop - half] = value
            else:
                qs[b, 0, :, start:half] = value[:, : half - start]
                qs[b, 1, :, : stop - half] = value[:, half - start :]

    first, second, third, fourth, fifth, sixth = ({} for _ in range(6))
    tiles = width // 2 // 128

    def send_core(b):
        first[b] = send(qs.at[b, 1 - c], qc.at[b], s1_s.at[b], s1_r.at[b], (x, y, z, 1 - c))

    def send_x(b):
        first[b].wait_recv()
        for t in range(4):
            xs[b, t] = qs[b, c, 8 * t : 8 * t + 8, :] + qc[b, 8 * t : 8 * t + 8, :]
        second[b] = [
            send(xs.at[b, px], xr.at[b, i], s2_s.at[b, i], s2_r.at[b, i], (px, y, z, c))
            for i, px in enumerate(x_peers)
        ]

    def send_z(b):
        value = xs[b, x]
        for i, copy in enumerate(second[b]):
            copy.wait_recv()
            value = value + xr[b, i]
        for t in range(tiles):
            zs[b, t] = value[:, t * 128 : (t + 1) * 128]
        zs[b, tiles] = jnp.zeros((8, 128), F32)
        third[b] = [
            send(zs.at[b, pz], zr.at[b, i], s3_s.at[b, i], s3_r.at[b, i], (x, y, pz, c))
            for i, pz in enumerate(z_peers)
        ]

    def back_z(b):
        value = zs[b, z]
        for i, copy in enumerate(third[b]):
            copy.wait_recv()
            value = value + zr[b, i]
        zg[b, z] = value * (1.0 / 64)
        fourth[b] = [
            send(zg.at[b, z], zg.at[b, z], s4_s.at[b, i], s4_r.at[b, i], (x, y, pz, c))
            for i, pz in enumerate(z_peers)
        ]

    def back_x(b):
        for copy in fourth[b]:
            copy.wait_recv()
        for t in range(tiles):
            qg[b, c, x, :, t * 128 : (t + 1) * 128] = zg[b, t]
        fifth[b] = [
            send(qg.at[b, c, x], qg.at[b, c, x], s5_s.at[b, i], s5_r.at[b, i], (px, y, z, c))
            for i, px in enumerate(x_peers)
        ]

    def back_core(b):
        for copy in fifth[b]:
            copy.wait_recv()
        sixth[b] = send(qg.at[b, c], qg.at[b, c], s6_s.at[b], s6_r.at[b], (x, y, z, 1 - c))

    local_t(0)
    send_core(0)
    local_t(1)
    send_x(0)
    send_core(1)
    local_t(2)
    send_x(1)
    send_core(2)
    send_x(2)
    gram = lax.dot_general(
        left, left_t, (((1,), (0,)), ((), ())), precision=HIGHEST, preferred_element_type=F32
    )
    packed = jnp.zeros((RANK, 128), F32)
    for b in range(BUCKETS):
        packed = jnp.where(lane // RANK == b, gram[b * RANK : (b + 1) * RANK, :], packed)
    done = jnp.zeros((RANK, 128), F32)
    packed, done = eliminate(packed, done, lane, 0, 8)
    packed, done = eliminate(packed, done, lane, 8, 16)
    for b in range(BUCKETS):
        send_z(b)
    packed, done = eliminate(packed, done, lane, 16, 24)
    packed, done = eliminate(packed, done, lane, 24, 32)
    row = lax.broadcasted_iota(jnp.int32, (RANK, 128), 0)
    inverse = jnp.where(lane % RANK <= row, done, 0.0)
    blocks = [jnp.where(lane // RANK == b, inverse, 0.0) for b in range(BUCKETS)]
    blocks.append(jnp.zeros((RANK, 128), F32))
    factor = jnp.concatenate(blocks, axis=0)
    for b in range(BUCKETS):
        back_z(b)
    basis_t = lax.dot_general(
        left_t[:ROWS], factor, (((1,), (1,)), ((), ())), precision=HIGHEST, preferred_element_type=F32
    )
    weight_t = lax.dot_general(
        basis_t, factor, (((1,), (0,)), ((), ())), precision=HIGHEST, preferred_element_type=F32
    )
    both = jnp.concatenate([weight_t, inverse], axis=0)
    for b in range(BUCKETS):
        high, low = split(both[:, b * RANK : (b + 1) * RANK])
        w_ref[b] = jnp.concatenate([high, low, high, jnp.zeros_like(high)], axis=1)
    for b in range(BUCKETS):
        back_x(b)
    for copy in sends[: -BUCKETS * len(XS)]:
        copy.wait_send()
    del sends[: -BUCKETS * len(XS)]
    for b in range(BUCKETS):
        back_core(b)
    half = width // 2
    for b in range(BUCKETS):
        sixth[b].wait_recv()
        for h in range(2):
            cols = slice(h * half, (h + 1) * half)
            high, low = split(jnp.concatenate([qg[b, h, t] for t in range(4)], axis=0))
            stacked = jnp.concatenate([high, high, low, jnp.zeros_like(high)], axis=0)
            both = dot(w_ref[b], stacked)
            q_ref[b, :, cols] = both[ROWS:]
            err_ref[0, b, :, cols] = c_ref[b, :, cols] - both[:ROWS]
    for copy in sends:
        copy.wait_send()


def per_device(gradient, error_memory, right_factor_initial):
    width = right_factor_initial.shape[2]
    corrected = gradient[0].astype(F32) + error_memory[0]
    half = width // 2
    dma = pltpu.SemaphoreType.DMA
    vmem = pltpu.VMEM
    whole = pl.BlockSpec(memory_space=pltpu.VMEM)
    b3 = BUCKETS
    n_xy, n_x, n_z = len(XY), NX - 1, NZ - 1
    return pl.pallas_call(
        reduce_kernel,
        out_shape=(
            jax.ShapeDtypeStruct((b3, RANK, width), F32),
            jax.ShapeDtypeStruct((1, b3, ROWS, width), F32),
        ),
        in_specs=[whole, whole],
        out_specs=(whole, whole),
        scratch_shapes=[
            vmem((b3, ROWS, width), BF16),
            vmem((b3, ROWS, width), BF16),
            vmem((256, width), BF16),
            vmem((b3, ROWS + RANK, 128), BF16),
            vmem((GROUP, PIECE, 128), F32),
            vmem((n_xy, PIECE, 128), F32),
            vmem((PIECE, 128), F32),
            vmem((PIECE, 128), F32),
            vmem((NZ, PIECE, 128), F32),
            vmem((GROUP, PIECE, 128), F32),
            vmem((256, 128), F32),
            vmem((b3, 2, RANK, half), F32),
            vmem((b3, RANK, half), F32),
            vmem((b3, 4, 8, half), F32),
            vmem((b3, n_x, 8, half), F32),
            vmem((b3, NZ, 8, 128), F32),
            vmem((b3, n_z, 8, 128), F32),
            vmem((b3, NZ, 8, 128), F32),
            vmem((b3, 2, 4, 8, half), F32),
            dma((n_xy,)), dma((n_xy,)),
            dma, dma,
            dma((n_z,)), dma((n_z,)),
            dma((n_xy,)), dma((n_xy,)),
            dma((b3,)), dma((b3,)),
            dma((b3, n_x)), dma((b3, n_x)),
            dma((b3, n_z)), dma((b3, n_z)),
            dma((b3, n_z)), dma((b3, n_z)),
            dma((b3, n_x)), dma((b3, n_x)),
            dma((b3,)), dma((b3,)),
        ],
        compiler_params=pltpu.CompilerParams(
            collective_id=0, has_side_effects=True, vmem_limit_bytes=32 << 20
        ),
        name="reduce_kernel",
    )(corrected, right_factor_initial)


def solution(mesh):
    placed = (P("dp", None, None, "mp"), P("dp", None, None, "mp"), P(None, None, "mp"))
    return jax.shard_map(
        per_device,
        mesh=mesh,
        in_specs=placed,
        out_specs=(P(None, None, "mp"), P("dp", None, None, "mp")),
        check_vma=False,
    )
```

time: 61.8 us -> 56.8 us (0.919)
  Pallas kernels: 56.1 us -> 50 us
  other arithmetic: 0 us -> 3.27 us
  local copies, waits for them, and re-layouts: 4.84 us -> 2.84 us
    pallas_call x2 -> x1, Pallas kernels: 56.1 us -> 50 us  [per_device(): pl.pallas_call(reduce_kernel, out_shape=(jax.ShapeDtypeStruct((b3, RANK,...]
    add x0 -> x1, other arithmetic: none -> 3.27 us  [per_device(): corrected = gradient[0].astype(F32) + error_memory[0]]
    unnamed x6 -> x4, local copies, waits for them, and re-layouts: 4.84 us -> 2.84 us
where the time goes in v2:
time: 56.8 us; the launch traced here: 56.7 us
  Pallas kernels  50 us (88%)
  other arithmetic  3.27 us (6%)
  local copies, waits for them, and re-layouts  2.84 us (5%)
  between operations  0.66 us (1%)
    pallas_call x1, Pallas kernels, per_device(): pl.pallas_call(reduce_kernel, out_shape=(jax.ShapeDtypeStruct((b3, RANK,...  50 us
    add x1, other arithmetic, per_device(): corrected = gradient[0].astype(F32) + error_memory[0]  3.27 us
    unnamed x4, local copies, waits for them, and re-layouts  2.84 us

profile of v2, /device:TPU:1, one launch (start us, length us, event | category | flops | bytes accessed | tf_op | source)
XLA Modules:
  0.0 56.7 jit_solution(12598219883377793571)
XLA Ops:
  0.6 0.0 copy-start
  0.6 3.3 %add_bitcast_fusion.c_ref = f32[3,192,1792]{2,1,0:T(8,128)S(1)} fusion(f32[1,3,192,1792]{3,2,1,0:T(8,128)} %param.4, bf16[1,3,192,1792]{3,2,1,0:T(8,128)(2,1)} %param.3), kind=kLoop, calls=%fused_computation | loop fusion | flops 2064384 | bytes 10321920 | tf_op jit(solution)/shard_map/add | solution.py:290
  3.9 0.0 copy-done
  3.9 50.0 %reduce_kernel.1 = (f32[3,32,1792]{2,1,0:T(8,128)S(1)}, f32[1,3,192,1792]{3,2,1,0:T(8,128)S(1)}) custom-call(f32[3,192,1792]{2,1,0:T(8,128)S(1)} %add_bitcast_fusion.c_ref, f32[3,32,1792]{2,1,0:T(8,128)S(1)} %copy-done), custom_call_target="tpu_custom_call" | custom-call | tf_op jit(solution)/shard_map/reduce_kernel/pallas_call | solution.py:297
  53.9 0.8 %copy.7 = f32[3,32,1792]{2,1,0:T(8,128)} copy(f32[3,32,1792]{2,1,0:T(8,128)S(1)} %get-tuple-element.4) | data formatting | bytes 1376256
  54.8 2.0 %copy.8 = f32[1,3,192,1792]{3,2,1,0:T(8,128)} copy(f32[1,3,192,1792]{3,2,1,0:T(8,128)S(1)} %get-tuple-element.5) | data formatting | bytes 8257536
Async XLA Ops:
  0.6 3.3 %copy-start = (f32[3,32,1792]{2,1,0:T(8,128)S(1)}, f32[3,32,1792]{2,1,0:T(8,128)}, u32[]{:S(2)}) copy-start(f32[3,32,1792]{2,1,0:T(8,128)} %r_ref.1) | copy-start | bytes 2064388

commit v3 on v2

--- a/solution.py
+++ b/solution.py
@@ -12,6 +12,8 @@
 BUCKETS, RANK, ROWS = 3, 32, 192
 GROUP = NX * NY
 PIECE = ROWS // GROUP
+PARTS = 9
+PART = BUCKETS * ROWS // PARTS
 HOPS = [0, 1, 2, 1]
 XY = sorted(
     ((i, j) for i in range(NX) for j in range(NY) if i or j), key=lambda p: -HOPS[p[0]] - HOPS[p[1]]
@@ -57,19 +59,28 @@
     return z, done
 
 
-def reduce_kernel(
-    c_ref, r_ref, q_ref, err_ref,
-    ch_ref, cl_ref, rr_ref, w_ref,
-    ps, pr, pcs, pcr, zp, pg, pf,
-    qs, qc, xs, xr, zs, zr, zg, qg,
-    pa_s, pa_r, pc_s, pc_r, pz_s, pz_r, pg_s, pg_r,
-    s1_s, s1_r, s2_s, s2_r, s3_s, s3_r, s4_s, s4_r, s5_s, s5_r, s6_s, s6_r,
-):
+def reduce_kernel(g_hbm, e_hbm, r_hbm, *refs):
+    q_refs, err_refs, refs = refs[:BUCKETS], refs[BUCKETS : BUCKETS + PARTS], refs[BUCKETS + PARTS :]
+    (
+        g_ref, c_ref, r_ref, ch_ref, cl_ref, rr_ref, w_ref,
+        ps, pr, pcs, pcr, zp, pg, pf,
+        qs, qc, xs, xr, zs, zr, zg, qg,
+        pa_s, pa_r, pc_s, pc_r, pz_s, pz_r, pg_s, pg_r,
+        s1_s, s1_r, s2_s, s2_r, s3_s, s3_r, s4_s, s4_r, s5_s, s5_r, s6_s, s6_r,
+        in_sem,
+    ) = refs
     x, y, z, c = place()
     xy_peers = [((x + i) % NX, (y + j) % NY) for i, j in XY]
     x_peers = [(x + i) % NX for i in XS]
     z_peers = [(z + i) % NZ for i in ZS]
     mine = x * NY + y
+
+    loads = [pltpu.make_async_copy(r_hbm, r_ref, in_sem.at[0])]
+    for b in range(BUCKETS):
+        loads.append(pltpu.make_async_copy(g_hbm.at[0, b], g_ref.at[b], in_sem.at[1 + 2 * b]))
+        loads.append(pltpu.make_async_copy(e_hbm.at[0, b], c_ref.at[b], in_sem.at[2 + 2 * b]))
+    for load in loads:
+        load.start()
 
     barrier = pltpu.get_barrier_semaphore()
     for px, py in xy_peers:
@@ -90,6 +101,7 @@
         return copy
 
     width = r_ref.shape[2]
+    loads[0].wait()
     rr_ref[...] = jnp.zeros_like(rr_ref)
     for b in range(BUCKETS):
         high, low = split(r_ref[b])
@@ -101,11 +113,14 @@
     step = 256
     total = jnp.zeros((ROWS, 128), F32)
     for b in range(BUCKETS):
+        loads[1 + 2 * b].wait()
+        loads[2 + 2 * b].wait()
         both = jnp.zeros((ROWS, 256), F32)
         rest = jnp.zeros((ROWS, 128), F32)
         for start in range(0, width, step):
             cols = slice(start, start + step)
-            value = c_ref[b, :, cols]
+            value = g_ref[b, :, cols].astype(F32) + c_ref[b, :, cols]
+            c_ref[b, :, cols] = value
             high, low = split(value)
             ch_ref[b, :, cols] = high
             cl_ref[b, :, cols] = low
@@ -225,15 +240,11 @@
             copy.wait_recv()
         sixth[b] = send(qg.at[b, c], qg.at[b, c], s6_s.at[b], s6_r.at[b], (x, y, z, 1 - c))
 
-    local_t(0)
-    send_core(0)
-    local_t(1)
-    send_x(0)
-    send_core(1)
-    local_t(2)
-    send_x(1)
-    send_core(2)
-    send_x(2)
+    for b in range(BUCKETS):
+        local_t(b)
+        send_core(b)
+    for b in range(BUCKETS):
+        send_x(b)
     gram = lax.dot_general(
         left, left_t, (((1,), (0,)), ((), ())), precision=HIGHEST, preferred_element_type=F32
     )
@@ -279,30 +290,50 @@
             high, low = split(jnp.concatenate([qg[b, h, t] for t in range(4)], axis=0))
             stacked = jnp.concatenate([high, high, low, jnp.zeros_like(high)], axis=0)
             both = dot(w_ref[b], stacked)
-            q_ref[b, :, cols] = both[ROWS:]
-            err_ref[0, b, :, cols] = c_ref[b, :, cols] - both[:ROWS]
+            q_refs[b][:, cols] = both[ROWS:]
+            for i in range(PARTS // BUCKETS):
+                rows = slice(i * PART, (i + 1) * PART)
+                err_refs[b * (PARTS // BUCKETS) + i][:, cols] = c_ref[b, rows, cols] - both[rows]
     for copy in sends:
         copy.wait_send()
 
 
+def store_kernel(*refs):
+    parts, (q_out, err_out, sem) = refs[:-3], refs[-3:]
+    copies = []
+    for i in range(PARTS):
+        b, row = divmod(i * PART, ROWS)
+        rows = pl.ds(row, PART)
+        copies.append(
+            pltpu.make_async_copy(parts[BUCKETS + i], err_out.at[0, b, rows], sem.at[BUCKETS + i])
+        )
+    for b in range(BUCKETS):
+        copies.append(pltpu.make_async_copy(parts[b], q_out.at[b], sem.at[b]))
+    for copy in copies:
+        copy.start()
+    for copy in copies:
+        copy.wait()
+
+
 def per_device(gradient, error_memory, right_factor_initial):
     width = right_factor_initial.shape[2]
-    corrected = gradient[0].astype(F32) + error_memory[0]
     half = width // 2
     dma = pltpu.SemaphoreType.DMA
     vmem = pltpu.VMEM
     whole = pl.BlockSpec(memory_space=pltpu.VMEM)
+    hbm = pl.BlockSpec(memory_space=pl.ANY)
     b3 = BUCKETS
     n_xy, n_x, n_z = len(XY), NX - 1, NZ - 1
-    return pl.pallas_call(
+    made = pl.pallas_call(
         reduce_kernel,
-        out_shape=(
-            jax.ShapeDtypeStruct((b3, RANK, width), F32),
-            jax.ShapeDtypeStruct((1, b3, ROWS, width), F32),
-        ),
-        in_specs=[whole, whole],
-        out_specs=(whole, whole),
+        out_shape=(jax.ShapeDtypeStruct((RANK, width), F32),) * b3
+        + (jax.ShapeDtypeStruct((PART, width), F32),) * PARTS,
+        in_specs=[hbm] * 3,
+        out_specs=(whole,) * (b3 + PARTS),
         scratch_shapes=[
+            vmem((b3, ROWS, width), BF16),
+            vmem((b3, ROWS, width), F32),
+            vmem((b3, RANK, width), F32),
             vmem((b3, ROWS, width), BF16),
             vmem((b3, ROWS, width), BF16),
             vmem((256, width), BF16),
@@ -332,12 +363,25 @@
             dma((b3, n_z)), dma((b3, n_z)),
             dma((b3, n_x)), dma((b3, n_x)),
             dma((b3,)), dma((b3,)),
+            dma((1 + 2 * b3,)),
         ],
         compiler_params=pltpu.CompilerParams(
-            collective_id=0, has_side_effects=True, vmem_limit_bytes=32 << 20
+            collective_id=0, has_side_effects=True, vmem_limit_bytes=49 << 20
         ),
         name="reduce_kernel",
-    )(corrected, right_factor_initial)
+    )(gradient, error_memory, right_factor_initial)
+    return pl.pallas_call(
+        store_kernel,
+        out_shape=(
+            jax.ShapeDtypeStruct((b3, RANK, width), F32),
+            jax.ShapeDtypeStruct((1, b3, ROWS, width), F32),
+        ),
+        in_specs=[hbm] * (b3 + PARTS),
+        out_specs=(hbm, hbm),
+        scratch_shapes=[dma((b3 + PARTS,))],
+        compiler_params=pltpu.CompilerParams(vmem_limit_bytes=1 << 20),
+        name="store_kernel",
+    )(*made)
 
 
 def solution(mesh):

time: 56.8 us -> 53 us (0.933)
  other arithmetic: 3.27 us -> 0 us
  local copies, waits for them, and re-layouts: 2.84 us -> 0 us
  Pallas kernels: 50 us -> 52.3 us
    add x1 -> x0, other arithmetic: 3.27 us -> none  [per_device(): corrected = gradient[0].astype(F32) + error_memory[0]]
    unnamed x4 -> x0, local copies, waits for them, and re-layouts: 2.84 us -> none
    pallas_call x1 -> x2, Pallas kernels: 50 us -> 52.3 us  [the longest x1 50 us: per_device(): pl.pallas_call(reduce_kernel, out_shape=(jax.ShapeDtypeStruct((RANK, widt...]
where the time goes in v3:
time: 53 us
  Pallas kernels  52.3 us (99%)
  between operations  0.64 us (1%)
    pallas_call x1, Pallas kernels, per_device(): pl.pallas_call(reduce_kernel, out_shape=(jax.ShapeDtypeStruct((RANK, widt...  50 us
    pallas_call x1, Pallas kernels, per_device(): pl.pallas_call(store_kernel, out_shape=(jax.ShapeDtypeStruct((b3, RANK, w...  2.3 us

profile of v3, /device:TPU:1, one launch (start us, length us, event | category | flops | bytes accessed | tf_op | source)
XLA Modules:
  0.0 53.0 jit_solution(5040118335763713702)
XLA Ops:
  0.6 50.0 %reduce_kernel.1 = (f32[32,1792]{1,0:T(8,128)S(1)}, f32[32,1792]{1,0:T(8,128)S(1)}, f32[32,1792]{1,0:T(8,128)S(1)}, f32[64,1792]{1,0:T(8,128)S(1)}, f32[64,1792]...) custom-call(bf16[1,3,192,1792]{3,2,1,0:T(8,128)(2,1)} %g_hbm.1, ...), custom_call_target="tpu_custom_call" | custom-call | tf_op jit(solution)/shard_map/reduce_kernel/pallas_call | solution.py:327
  50.7 2.3 %store_kernel.1 = (f32[3,32,1792]{2,1,0:T(8,128)}, f32[1,3,192,1792]{3,2,1,0:T(8,128)}) custom-call(f32[32,1792]{1,0:T(8,128)S(1)} %get-tuple-element.14.refs_0_, f32[32,1792]{1,0:T(8,128)S(1)} %get-tuple-element.15.refs_1_, f32[32,1792]{1,0:T(8,128)S(1)} %get-tuple-element.16.refs_2_, f32[64,1792]{1,0:T(8,128)S(1)} %get-tuple-element.17.refs_3_, ...), custom_call_target="tpu_custom_call" | custom-call | tf_op jit(solution)/shard_map/store_kernel/pallas_call | solution.py:373

commit v4 on v3

--- a/solution.py
+++ b/solution.py
@@ -89,16 +89,14 @@
         pl.semaphore_signal(barrier, inc=1, device_id=device(x, y, pz, c), device_id_type=MESH)
     pl.semaphore_signal(barrier, inc=1, device_id=device(x, y, z, 1 - c), device_id_type=MESH)
 
-    sends = []
-
     def send(src, dst, send_sem, recv_sem, where):
-        copy = pltpu.make_async_remote_copy(
+        pltpu.make_async_remote_copy(
             src_ref=src, dst_ref=dst, send_sem=send_sem, recv_sem=recv_sem,
             device_id=device(*where), device_id_type=MESH,
-        )
-        copy.start()
-        sends.append(copy)
-        return copy
+        ).start()
+
+    def wait(like, sem):
+        pltpu.make_async_copy(like, like, sem).wait()
 
     width = r_ref.shape[2]
     loads[0].wait()
@@ -134,34 +132,26 @@
 
     pl.semaphore_wait(barrier, len(XY) + NZ)
 
-    copies = [
-        send(ps.at[px * NY + py], pr.at[i], pa_s.at[i], pa_r.at[i], (px, py, z, c))
-        for i, (px, py) in enumerate(xy_peers)
-    ]
+    for i, (px, py) in enumerate(xy_peers):
+        send(ps.at[px * NY + py], pr.at[i], pa_s, pa_r, (px, py, z, c))
     piece = ps[mine]
-    for i, copy in enumerate(copies):
-        copy.wait_recv()
+    wait(pr, pa_r)
+    for i in range(len(XY)):
         piece = piece + pr[i]
     pcs[...] = piece
-    copy = send(pcs, pcr, pc_s, pc_r, (x, y, z, 1 - c))
-    copy.wait_recv()
-    piece = piece + pcr[...]
-    zp[z] = piece
-    copies = [
-        send(zp.at[z], zp.at[z], pz_s.at[i], pz_r.at[i], (x, y, at, c)) for i, at in enumerate(z_peers)
-    ]
-    for copy in copies:
-        copy.wait_recv()
+    send(pcs, pcr, pc_s, pc_r, (x, y, z, 1 - c))
+    wait(pcr, pc_r)
+    zp[z] = piece + pcr[...]
+    for pz in z_peers:
+        send(zp.at[z], zp.at[z], pz_s, pz_r, (x, y, pz, c))
+    wait(zp.at[: NZ - 1], pz_r)
     piece = zp[0]
     for i in range(1, NZ):
         piece = piece + zp[i]
     pg[mine] = piece
-    copies = [
-        send(pg.at[mine], pg.at[mine], pg_s.at[i], pg_r.at[i], (px, py, z, c))
-        for i, (px, py) in enumerate(xy_peers)
-    ]
-    for copy in copies:
-        copy.wait_recv()
+    for px, py in xy_peers:
+        send(pg.at[mine], pg.at[mine], pg_s, pg_r, (px, py, z, c))
+    wait(pg.at[: GROUP - 1], pg_r)
     for i in range(GROUP):
         pf[i * PIECE : (i + 1) * PIECE, :] = pg[i]
     pf[ROWS:, :] = jnp.zeros((256 - ROWS, 128), F32)
@@ -186,59 +176,48 @@
                 qs[b, 0, :, start:half] = value[:, : half - start]
                 qs[b, 1, :, : stop - half] = value[:, half - start :]
 
-    first, second, third, fourth, fifth, sixth = ({} for _ in range(6))
     tiles = width // 2 // 128
 
     def send_core(b):
-        first[b] = send(qs.at[b, 1 - c], qc.at[b], s1_s.at[b], s1_r.at[b], (x, y, z, 1 - c))
+        send(qs.at[b, 1 - c], qc.at[b], s1_s.at[b], s1_r.at[b], (x, y, z, 1 - c))
 
     def send_x(b):
-        first[b].wait_recv()
+        wait(qc.at[b], s1_r.at[b])
         for t in range(4):
             xs[b, t] = qs[b, c, 8 * t : 8 * t + 8, :] + qc[b, 8 * t : 8 * t + 8, :]
-        second[b] = [
-            send(xs.at[b, px], xr.at[b, i], s2_s.at[b, i], s2_r.at[b, i], (px, y, z, c))
-            for i, px in enumerate(x_peers)
-        ]
+        for i, px in enumerate(x_peers):
+            send(xs.at[b, px], xr.at[b, i], s2_s.at[b], s2_r.at[b], (px, y, z, c))
 
     def send_z(b):
         value = xs[b, x]
-        for i, copy in enumerate(second[b]):
-            copy.wait_recv()
+        wait(xr.at[b], s2_r.at[b])
+        for i in range(NX - 1):
             value = value + xr[b, i]
         for t in range(tiles):
             zs[b, t] = value[:, t * 128 : (t + 1) * 128]
         zs[b, tiles] = jnp.zeros((8, 128), F32)
-        third[b] = [
-            send(zs.at[b, pz], zr.at[b, i], s3_s.at[b, i], s3_r.at[b, i], (x, y, pz, c))
-            for i, pz in enumerate(z_peers)
-        ]
+        for i, pz in enumerate(z_peers):
+            send(zs.at[b, pz], zr.at[b, i], s3_s.at[b], s3_r.at[b], (x, y, pz, c))
 
     def back_z(b):
         value = zs[b, z]
-        for i, copy in enumerate(third[b]):
-            copy.wait_recv()
+        wait(zr.at[b], s3_r.at[b])
+        for i in range(NZ - 1):
             value = value + zr[b, i]
         zg[b, z] = value * (1.0 / 64)
-        fourth[b] = [
-            send(zg.at[b, z], zg.at[b, z], s4_s.at[b, i], s4_r.at[b, i], (x, y, pz, c))
-            for i, pz in enumerate(z_peers)
-        ]
+        for pz in z_peers:
+            send(zg.at[b, z], zg.at[b, z], s4_s.at[b], s4_r.at[b], (x, y, pz, c))
 
     def back_x(b):
-        for copy in fourth[b]:
-            copy.wait_recv()
+        wait(zg.at[b, : NZ - 1], s4_r.at[b])
         for t in range(tiles):
             qg[b, c, x, :, t * 128 : (t + 1) * 128] = zg[b, t]
-        fifth[b] = [
-            send(qg.at[b, c, x], qg.at[b, c, x], s5_s.at[b, i], s5_r.at[b, i], (px, y, z, c))
-            for i, px in enumerate(x_peers)
-        ]
+        for px in x_peers:
+            send(qg.at[b, c, x], qg.at[b, c, x], s5_s.at[b], s5_r.at[b], (px, y, z, c))
 
     def back_core(b):
-        for copy in fifth[b]:
-            copy.wait_recv()
-        sixth[b] = send(qg.at[b, c], qg.at[b, c], s6_s.at[b], s6_r.at[b], (x, y, z, 1 - c))
+        wait(qg.at[b, c, : NX - 1], s5_r.at[b])
+        send(qg.at[b, c], qg.at[b, c], s6_s.at[b], s6_r.at[b], (x, y, z, 1 - c))
 
     for b in range(BUCKETS):
         local_t(b)
@@ -277,14 +256,20 @@
         w_ref[b] = jnp.concatenate([high, low, high, jnp.zeros_like(high)], axis=1)
     for b in range(BUCKETS):
         back_x(b)
-    for copy in sends[: -BUCKETS * len(XS)]:
-        copy.wait_send()
-    del sends[: -BUCKETS * len(XS)]
+    wait(pr, pa_s)
+    wait(pcs, pc_s)
+    wait(zp.at[: NZ - 1], pz_s)
+    wait(pg.at[: GROUP - 1], pg_s)
+    for b in range(BUCKETS):
+        wait(qc.at[b], s1_s.at[b])
+        wait(xr.at[b], s2_s.at[b])
+        wait(zr.at[b], s3_s.at[b])
+        wait(zg.at[b, : NZ - 1], s4_s.at[b])
     for b in range(BUCKETS):
         back_core(b)
     half = width // 2
     for b in range(BUCKETS):
-        sixth[b].wait_recv()
+        wait(qg.at[b, 1 - c], s6_r.at[b])
         for h in range(2):
             cols = slice(h * half, (h + 1) * half)
             high, low = split(jnp.concatenate([qg[b, h, t] for t in range(4)], axis=0))
@@ -294,8 +279,9 @@
             for i in range(PARTS // BUCKETS):
                 rows = slice(i * PART, (i + 1) * PART)
                 err_refs[b * (PARTS // BUCKETS) + i][:, cols] = c_ref[b, rows, cols] - both[rows]
-    for copy in sends:
-        copy.wait_send()
+    for b in range(BUCKETS):
+        wait(qg.at[b, c, : NX - 1], s5_s.at[b])
+        wait(qg.at[b, c], s6_s.at[b])
 
 
 def store_kernel(*refs):
@@ -353,16 +339,8 @@
             vmem((b3, n_z, 8, 128), F32),
             vmem((b3, NZ, 8, 128), F32),
             vmem((b3, 2, 4, 8, half), F32),
-            dma((n_xy,)), dma((n_xy,)),
-            dma, dma,
-            dma((n_z,)), dma((n_z,)),
-            dma((n_xy,)), dma((n_xy,)),
-            dma((b3,)), dma((b3,)),
-            dma((b3, n_x)), dma((b3, n_x)),
-            dma((b3, n_z)), dma((b3, n_z)),
-            dma((b3, n_z)), dma((b3, n_z)),
-            dma((b3, n_x)), dma((b3, n_x)),
-            dma((b3,)), dma((b3,)),
+            *([dma] * 8),
+            *([dma((b3,))] * 12),
             dma((1 + 2 * b3,)),
         ],
         compiler_params=pltpu.CompilerParams(

time: 53 us -> 51.4 us (0.970)
  Pallas kernels: 52.3 us -> 50.7 us
    pallas_call x1, Pallas kernels: 50 us -> 48.4 us  [per_device(): pl.pallas_call(reduce_kernel, out_shape=(jax.ShapeDtypeStruct((RANK, widt...]
where the time goes in v4:
time: 51.4 us
  Pallas kernels  50.7 us (99%)
  between operations  0.64 us (1%)
    pallas_call x1, Pallas kernels, per_device(): pl.pallas_call(reduce_kernel, out_shape=(jax.ShapeDtypeStruct((RANK, widt...  48.4 us
    pallas_call x1, Pallas kernels, per_device(): pl.pallas_call(store_kernel, out_shape=(jax.ShapeDtypeStruct((b3, RANK, w...  2.3 us

profile of v4, /device:TPU:1, one launch (start us, length us, event | category | flops | bytes accessed | tf_op | source)
XLA Modules:
  0.0 51.4 jit_solution(3770532603724843569)
XLA Ops:
  0.6 48.4 %reduce_kernel.1 = (f32[32,1792]{1,0:T(8,128)S(1)}, f32[32,1792]{1,0:T(8,128)S(1)}, f32[32,1792]{1,0:T(8,128)S(1)}, f32[64,1792]{1,0:T(8,128)S(1)}, f32[64,1792]...) custom-call(bf16[1,3,192,1792]{3,2,1,0:T(8,128)(2,1)} %g_hbm.1, ...), custom_call_target="tpu_custom_call" | custom-call | tf_op jit(solution)/shard_map/reduce_kernel/pallas_call | solution.py:313
  49.1 2.3 %store_kernel.1 = (f32[3,32,1792]{2,1,0:T(8,128)}, f32[1,3,192,1792]{3,2,1,0:T(8,128)}) custom-call(f32[32,1792]{1,0:T(8,128)S(1)} %get-tuple-element.14.refs_0_, f32[32,1792]{1,0:T(8,128)S(1)} %get-tuple-element.15.refs_1_, f32[32,1792]{1,0:T(8,128)S(1)} %get-tuple-element.16.refs_2_, f32[64,1792]{1,0:T(8,128)S(1)} %get-tuple-element.17.refs_3_, ...), custom_call_target="tpu_custom_call" | custom-call | tf_op jit(solution)/shard_map/store_kernel/pallas_call | solution.py:351

commit v5 on v4

--- a/solution.py
+++ b/solution.py
@@ -67,7 +67,7 @@
         qs, qc, xs, xr, zs, zr, zg, qg,
         pa_s, pa_r, pc_s, pc_r, pz_s, pz_r, pg_s, pg_r,
         s1_s, s1_r, s2_s, s2_r, s3_s, s3_r, s4_s, s4_r, s5_s, s5_r, s6_s, s6_r,
-        in_sem,
+        in_sem, fzs, fzr, fxs, fxr, fxg, fzg,
     ) = refs
     x, y, z, c = place()
     xy_peers = [((x + i) % NX, (y + j) % NY) for i, j in XY]
@@ -215,6 +215,41 @@
         for px in x_peers:
             send(qg.at[b, c, x], qg.at[b, c, x], s5_s.at[b], s5_r.at[b], (px, y, z, c))
 
+    def send_z_first():
+        wait(qc.at[0], s1_r.at[0])
+        for t in range(tiles):
+            cols = slice(t * 128, (t + 1) * 128)
+            fzs[t] = qs[0, c, :, cols] + qc[0, :, cols]
+        fzs[tiles] = jnp.zeros((RANK, 128), F32)
+        for i, pz in enumerate(z_peers):
+            send(fzs.at[pz], fzr.at[i], s2_s.at[0], s2_r.at[0], (x, y, pz, c))
+
+    def send_x_second():
+        value = fzs[z]
+        wait(fzr, s2_r.at[0])
+        for i in range(NZ - 1):
+            value = value + fzr[i]
+        for t in range(NX):
+            fxs[t] = value[8 * t : 8 * t + 8, :]
+        for i, px in enumerate(x_peers):
+            send(fxs.at[px], fxr.at[i], s3_s.at[0], s3_r.at[0], (px, y, z, c))
+
+    def back_x_second():
+        value = fxs[x]
+        wait(fxr, s3_r.at[0])
+        for i in range(NX - 1):
+            value = value + fxr[i]
+        fxg[x] = value * (1.0 / 64)
+        for px in x_peers:
+            send(fxg.at[x], fxg.at[x], s4_s.at[0], s4_r.at[0], (px, y, z, c))
+
+    def back_z_first():
+        wait(fxg.at[: NX - 1], s4_r.at[0])
+        for t in range(NX):
+            fzg[z, 8 * t : 8 * t + 8, :] = fxg[t]
+        for pz in z_peers:
+            send(fzg.at[z], fzg.at[z], s5_s.at[0], s5_r.at[0], (x, y, pz, c))
+
     def back_core(b):
         wait(qg.at[b, c, : NX - 1], s5_r.at[b])
         send(qg.at[b, c], qg.at[b, c], s6_s.at[b], s6_r.at[b], (x, y, z, 1 - c))
@@ -222,7 +257,8 @@
     for b in range(BUCKETS):
         local_t(b)
         send_core(b)
-    for b in range(BUCKETS):
+    send_z_first()
+    for b in range(1, BUCKETS):
         send_x(b)
     gram = lax.dot_general(
         left, left_t, (((1,), (0,)), ((), ())), precision=HIGHEST, preferred_element_type=F32
@@ -233,8 +269,9 @@
     done = jnp.zeros((RANK, 128), F32)
     packed, done = eliminate(packed, done, lane, 0, 8)
     packed, done = eliminate(packed, done, lane, 8, 16)
-    for b in range(BUCKETS):
+    for b in range(1, BUCKETS):
         send_z(b)
+    send_x_second()
     packed, done = eliminate(packed, done, lane, 16, 24)
     packed, done = eliminate(packed, done, lane, 24, 32)
     row = lax.broadcasted_iota(jnp.int32, (RANK, 128), 0)
@@ -242,8 +279,9 @@
     blocks = [jnp.where(lane // RANK == b, inverse, 0.0) for b in range(BUCKETS)]
     blocks.append(jnp.zeros((RANK, 128), F32))
     factor = jnp.concatenate(blocks, axis=0)
-    for b in range(BUCKETS):
+    for b in range(1, BUCKETS):
         back_z(b)
+    back_x_second()
     basis_t = lax.dot_general(
         left_t[:ROWS], factor, (((1,), (1,)), ((), ())), precision=HIGHEST, preferred_element_type=F32
     )
@@ -254,7 +292,8 @@
     for b in range(BUCKETS):
         high, low = split(both[:, b * RANK : (b + 1) * RANK])
         w_ref[b] = jnp.concatenate([high, low, high, jnp.zeros_like(high)], axis=1)
-    for b in range(BUCKETS):
+    back_z_first()
+    for b in range(1, BUCKETS):
         back_x(b)
     wait(pr, pa_s)
     wait(pcs, pc_s)
@@ -262,13 +301,18 @@
     wait(pg.at[: GROUP - 1], pg_s)
     for b in range(BUCKETS):
         wait(qc.at[b], s1_s.at[b])
-        wait(xr.at[b], s2_s.at[b])
-        wait(zr.at[b], s3_s.at[b])
-        wait(zg.at[b, : NZ - 1], s4_s.at[b])
-    for b in range(BUCKETS):
+        wait(xr.at[b] if b else fzr, s2_s.at[b])
+        wait(zr.at[b] if b else fxr, s3_s.at[b])
+        wait(zg.at[b, : NZ - 1] if b else fxg.at[: NX - 1], s4_s.at[b])
+    for b in range(1, BUCKETS):
         back_core(b)
+    wait(fzg.at[: NZ - 1], s5_r.at[0])
+    for t in range(tiles):
+        for i in range(NX):
+            qg[0, c, i, :, t * 128 : (t + 1) * 128] = fzg[t, 8 * i : 8 * i + 8, :]
+    send(qg.at[0, c], qg.at[0, c], s6_s.at[0], s6_r.at[0], (x, y, z, 1 - c))
     half = width // 2
-    for b in range(BUCKETS):
+    for b in (1, 2, 0):
         wait(qg.at[b, 1 - c], s6_r.at[b])
         for h in range(2):
             cols = slice(h * half, (h + 1) * half)
@@ -280,7 +324,7 @@
                 rows = slice(i * PART, (i + 1) * PART)
                 err_refs[b * (PARTS // BUCKETS) + i][:, cols] = c_ref[b, rows, cols] - both[rows]
     for b in range(BUCKETS):
-        wait(qg.at[b, c, : NX - 1], s5_s.at[b])
+        wait(qg.at[b, c, : NX - 1] if b else fzg.at[: NZ - 1], s5_s.at[b])
         wait(qg.at[b, c], s6_s.at[b])
 
 
@@ -342,6 +386,12 @@
             *([dma] * 8),
             *([dma((b3,))] * 12),
             dma((1 + 2 * b3,)),
+            vmem((NZ, RANK, 128), F32),
+            vmem((n_z, RANK, 128), F32),
+            vmem((NX, 8, 128), F32),
+            vmem((n_x, 8, 128), F32),
+            vmem((NX, 8, 128), F32),
+            vmem((NZ, RANK, 128), F32),
         ],
         compiler_params=pltpu.CompilerParams(
             collective_id=0, has_side_effects=True, vmem_limit_bytes=49 << 20

time: 51.4 us -> 50.3 us (0.979)
  Pallas kernels: 50.7 us -> 49.5 us
    pallas_call x1, Pallas kernels: 48.4 us -> 47.2 us  [per_device(): pl.pallas_call(reduce_kernel, out_shape=(jax.ShapeDtypeStruct((RANK, widt...]
where the time goes in v5:
time: 50.3 us; the launch traced here: 50.2 us
  Pallas kernels  49.5 us (98%)
  between operations  0.64 us (1%)
    pallas_call x1, Pallas kernels, per_device(): pl.pallas_call(reduce_kernel, out_shape=(jax.ShapeDtypeStruct((RANK, widt...  47.2 us
    pallas_call x1, Pallas kernels, per_device(): pl.pallas_call(store_kernel, out_shape=(jax.ShapeDtypeStruct((b3, RANK, w...  2.3 us

profile of v5, /device:TPU:1, one launch (start us, length us, event | category | flops | bytes accessed | tf_op | source)
XLA Modules:
  0.0 50.2 jit_solution(17355442653705498402)
XLA Ops:
  0.6 47.2 %reduce_kernel.1 = (f32[32,1792]{1,0:T(8,128)S(1)}, f32[32,1792]{1,0:T(8,128)S(1)}, f32[32,1792]{1,0:T(8,128)S(1)}, f32[64,1792]{1,0:T(8,128)S(1)}, f32[64,1792]...) custom-call(bf16[1,3,192,1792]{3,2,1,0:T(8,128)(2,1)} %g_hbm.1, ...), custom_call_target="tpu_custom_call" | custom-call | tf_op jit(solution)/shard_map/reduce_kernel/pallas_call | solution.py:357
  47.9 2.3 %store_kernel.1 = (f32[3,32,1792]{2,1,0:T(8,128)}, f32[1,3,192,1792]{3,2,1,0:T(8,128)}) custom-call(f32[32,1792]{1,0:T(8,128)S(1)} %get-tuple-element.14.refs_0_, f32[32,1792]{1,0:T(8,128)S(1)} %get-tuple-element.15.refs_1_, f32[32,1792]{1,0:T(8,128)S(1)} %get-tuple-element.16.refs_2_, f32[64,1792]{1,0:T(8,128)S(1)} %get-tuple-element.17.refs_3_, ...), custom_call_target="tpu_custom_call" | custom-call | tf_op jit(solution)/shard_map/store_kernel/pallas_call | solution.py:401

commit v6 on v5

--- a/solution.py
+++ b/solution.py
@@ -64,7 +64,7 @@
     (
         g_ref, c_ref, r_ref, ch_ref, cl_ref, rr_ref, w_ref,
         ps, pr, pcs, pcr, zp, pg, pf,
-        qs, qc, xs, xr, zs, zr, zg, qg,
+        qc, xs, xr, zs, zr, zg, qg,
         pa_s, pa_r, pc_s, pc_r, pz_s, pz_r, pg_s, pg_r,
         s1_s, s1_r, s2_s, s2_r, s3_s, s3_r, s4_s, s4_r, s5_s, s5_r, s6_s, s6_r,
         in_sem, fzs, fzr, fxs, fxr, fxg, fzg,
@@ -120,8 +120,6 @@
             value = g_ref[b, :, cols].astype(F32) + c_ref[b, :, cols]
             c_ref[b, :, cols] = value
             high, low = split(value)
-            ch_ref[b, :, cols] = high
-            cl_ref[b, :, cols] = low
             both = both + dot(high, rr_ref[:, cols], ((1,), (1,)))
             rest = rest + dot(low, rr_ref[:128, cols], ((1,), (1,)))
         part = both[:, :128] + both[:, 128:] + rest
@@ -134,6 +132,11 @@
 
     for i, (px, py) in enumerate(xy_peers):
         send(ps.at[px * NY + py], pr.at[i], pa_s, pa_r, (px, py, z, c))
+    half = width // 2
+    own = pl.ds(pl.multiple_of(c * half, 128), half)
+    other = pl.ds(pl.multiple_of((1 - c) * half, 128), half)
+    for b in range(BUCKETS):
+        send(c_ref.at[b, :, other], qc.at[b], s1_s.at[b], s1_r.at[b], (x, y, z, 1 - c))
     piece = ps[mine]
     wait(pr, pa_r)
     for i in range(len(XY)):
@@ -144,6 +147,16 @@
     zp[z] = piece + pcr[...]
     for pz in z_peers:
         send(zp.at[z], zp.at[z], pz_s, pz_r, (x, y, pz, c))
+    for b in range(BUCKETS):
+        wait(qc.at[b], s1_r.at[b])
+
+        @pl.loop(0, ROWS // 16)
+        def _(i):
+            rows = pl.ds(pl.multiple_of(i * 16, 16), 16)
+            high, low = split(c_ref[b, rows, own] + qc[b, rows, :])
+            ch_ref[b, rows, :] = high
+            cl_ref[b, rows, :] = low
+
     wait(zp.at[: NZ - 1], pz_r)
     piece = zp[0]
     for i in range(1, NZ):
@@ -163,28 +176,20 @@
     def local_t(b):
         rows = slice(b * RANK, (b + 1) * RANK)
         stacked = jnp.concatenate([left_high[rows], left_low[rows]], axis=0)
-        half = width // 2
-        for start in range(0, width, 256):
-            stop = start + 256
+        for start in range(0, half, 256):
+            stop = min(start + 256, half)
             one = dot(stacked, ch_ref[b, :, start:stop])
             value = one[:RANK] + one[RANK:] + dot(left_high[rows], cl_ref[b, :, start:stop])
-            if stop <= half:
-                qs[b, 0, :, start:stop] = value
-            elif start >= half:
-                qs[b, 1, :, start - half : stop - half] = value
+            if b == 0:
+                for t in range(start // 128, stop // 128):
+                    fzs[t] = value[:, t * 128 - start : t * 128 - start + 128]
             else:
-                qs[b, 0, :, start:half] = value[:, : half - start]
-                qs[b, 1, :, : stop - half] = value[:, half - start :]
+                for t in range(NX):
+                    xs[b, t, :, start:stop] = value[8 * t : 8 * t + 8, :]
 
     tiles = width // 2 // 128
 
-    def send_core(b):
-        send(qs.at[b, 1 - c], qc.at[b], s1_s.at[b], s1_r.at[b], (x, y, z, 1 - c))
-
     def send_x(b):
-        wait(qc.at[b], s1_r.at[b])
-        for t in range(4):
-            xs[b, t] = qs[b, c, 8 * t : 8 * t + 8, :] + qc[b, 8 * t : 8 * t + 8, :]
         for i, px in enumerate(x_peers):
             send(xs.at[b, px], xr.at[b, i], s2_s.at[b], s2_r.at[b], (px, y, z, c))
 
@@ -216,10 +221,6 @@
             send(qg.at[b, c, x], qg.at[b, c, x], s5_s.at[b], s5_r.at[b], (px, y, z, c))
 
     def send_z_first():
-        wait(qc.at[0], s1_r.at[0])
-        for t in range(tiles):
-            cols = slice(t * 128, (t + 1) * 128)
-            fzs[t] = qs[0, c, :, cols] + qc[0, :, cols]
         fzs[tiles] = jnp.zeros((RANK, 128), F32)
         for i, pz in enumerate(z_peers):
             send(fzs.at[pz], fzr.at[i], s2_s.at[0], s2_r.at[0], (x, y, pz, c))
@@ -254,11 +255,10 @@
         wait(qg.at[b, c, : NX - 1], s5_r.at[b])
         send(qg.at[b, c], qg.at[b, c], s6_s.at[b], s6_r.at[b], (x, y, z, 1 - c))
 
-    for b in range(BUCKETS):
-        local_t(b)
-        send_core(b)
+    local_t(0)
     send_z_first()
     for b in range(1, BUCKETS):
+        local_t(b)
         send_x(b)
     gram = lax.dot_general(
         left, left_t, (((1,), (0,)), ((), ())), precision=HIGHEST, preferred_element_type=F32
@@ -364,8 +364,8 @@
             vmem((b3, ROWS, width), BF16),
             vmem((b3, ROWS, width), F32),
             vmem((b3, RANK, width), F32),
-            vmem((b3, ROWS, width), BF16),
-            vmem((b3, ROWS, width), BF16),
+            vmem((b3, ROWS, half), BF16),
+            vmem((b3, ROWS, half), BF16),
             vmem((256, width), BF16),
             vmem((b3, ROWS + RANK, 128), BF16),
             vmem((GROUP, PIECE, 128), F32),
@@ -375,8 +375,7 @@
             vmem((NZ, PIECE, 128), F32),
             vmem((GROUP, PIECE, 128), F32),
             vmem((256, 128), F32),
-            vmem((b3, 2, RANK, half), F32),
-            vmem((b3, RANK, half), F32),
+            vmem((b3, ROWS, half), F32),
             vmem((b3, 4, 8, half), F32),
             vmem((b3, n_x, 8, half), F32),
             vmem((b3, NZ, 8, 128), F32),

time: 50.3 us -> 48.8 us (0.970)
  Pallas kernels: 49.5 us -> 48.1 us
    pallas_call x1, Pallas kernels: 47.2 us -> 45.8 us  [per_device(): pl.pallas_call(reduce_kernel, out_shape=(jax.ShapeDtypeStruct((RANK, widt...]
where the time goes in v6:
time: 48.8 us; the launch traced here: 48.7 us
  Pallas kernels  48.1 us (99%)
  between operations  0.64 us (1%)
    pallas_call x1, Pallas kernels, per_device(): pl.pallas_call(reduce_kernel, out_shape=(jax.ShapeDtypeStruct((RANK, widt...  45.8 us
    pallas_call x1, Pallas kernels, per_device(): pl.pallas_call(store_kernel, out_shape=(jax.ShapeDtypeStruct((b3, RANK, w...  2.3 us

profile of v6, /device:TPU:1, one launch (start us, length us, event | category | flops | bytes accessed | tf_op | source)
XLA Modules:
  0.0 48.7 jit_solution(6640891762899195990)
XLA Ops:
  0.6 45.8 %reduce_kernel.1 = (f32[32,1792]{1,0:T(8,128)S(1)}, f32[32,1792]{1,0:T(8,128)S(1)}, f32[32,1792]{1,0:T(8,128)S(1)}, f32[64,1792]{1,0:T(8,128)S(1)}, f32[64,1792]...) custom-call(bf16[1,3,192,1792]{3,2,1,0:T(8,128)(2,1)} %g_hbm.1, ...), custom_call_target="tpu_custom_call" | custom-call | tf_op jit(solution)/shard_map/reduce_kernel/pallas_call | solution.py:357
  46.4 2.3 %store_kernel.1 = (f32[3,32,1792]{2,1,0:T(8,128)}, f32[1,3,192,1792]{3,2,1,0:T(8,128)}) custom-call(f32[32,1792]{1,0:T(8,128)S(1)} %get-tuple-element.14.refs_0_, f32[32,1792]{1,0:T(8,128)S(1)} %get-tuple-element.15.refs_1_, f32[32,1792]{1,0:T(8,128)S(1)} %get-tuple-element.16.refs_2_, f32[64,1792]{1,0:T(8,128)S(1)} %get-tuple-element.17.refs_3_, ...), custom_call_target="tpu_custom_call" | custom-call | tf_op jit(solution)/shard_map/store_kernel/pallas_call | solution.py:400

commit v7 on v6

--- a/solution.py
+++ b/solution.py
@@ -65,9 +65,9 @@
         g_ref, c_ref, r_ref, ch_ref, cl_ref, rr_ref, w_ref,
         ps, pr, pcs, pcr, zp, pg, pf,
         qc, xs, xr, zs, zr, zg, qg,
-        pa_s, pa_r, pc_s, pc_r, pz_s, pz_r, pg_s, pg_r,
+        pa_s, pa_r, pc_r, pz_r, pg_r,
         s1_s, s1_r, s2_s, s2_r, s3_s, s3_r, s4_s, s4_r, s5_s, s5_r, s6_s, s6_r,
-        in_sem, fzs, fzr, fxs, fxr, fxg, fzg,
+        in_sem, like, fzs, fzr, fxs, fxr, fxg, fzg,
     ) = refs
     x, y, z, c = place()
     xy_peers = [((x + i) % NX, (y + j) % NY) for i, j in XY]
@@ -95,8 +95,8 @@
             device_id=device(*where), device_id_type=MESH,
         ).start()
 
-    def wait(like, sem):
-        pltpu.make_async_copy(like, like, sem).wait()
+    def wait(ref, sem):
+        pltpu.make_async_copy(ref, ref, sem).wait()
 
     width = r_ref.shape[2]
     loads[0].wait()
@@ -136,19 +136,19 @@
     own = pl.ds(pl.multiple_of(c * half, 128), half)
     other = pl.ds(pl.multiple_of((1 - c) * half, 128), half)
     for b in range(BUCKETS):
-        send(c_ref.at[b, :, other], qc.at[b], s1_s.at[b], s1_r.at[b], (x, y, z, 1 - c))
+        send(c_ref.at[b, :, other], qc.at[b], s1_s, s1_r, (x, y, z, 1 - c))
     piece = ps[mine]
     wait(pr, pa_r)
     for i in range(len(XY)):
         piece = piece + pr[i]
     pcs[...] = piece
-    send(pcs, pcr, pc_s, pc_r, (x, y, z, 1 - c))
+    send(pcs, pcr, pa_s, pc_r, (x, y, z, 1 - c))
     wait(pcr, pc_r)
     zp[z] = piece + pcr[...]
     for pz in z_peers:
-        send(zp.at[z], zp.at[z], pz_s, pz_r, (x, y, pz, c))
-    for b in range(BUCKETS):
-        wait(qc.at[b], s1_r.at[b])
+        send(zp.at[z], zp.at[z], pa_s, pz_r, (x, y, pz, c))
+    wait(qc, s1_r)
+    for b in range(BUCKETS):
 
         @pl.loop(0, ROWS // 16)
         def _(i):
@@ -163,7 +163,7 @@
         piece = piece + zp[i]
     pg[mine] = piece
     for px, py in xy_peers:
-        send(pg.at[mine], pg.at[mine], pg_s, pg_r, (px, py, z, c))
+        send(pg.at[mine], pg.at[mine], pa_s, pg_r, (px, py, z, c))
     wait(pg.at[: GROUP - 1], pg_r)
     for i in range(GROUP):
         pf[i * PIECE : (i + 1) * PIECE, :] = pg[i]
@@ -295,12 +295,9 @@
     back_z_first()
     for b in range(1, BUCKETS):
         back_x(b)
-    wait(pr, pa_s)
-    wait(pcs, pc_s)
-    wait(zp.at[: NZ - 1], pz_s)
-    wait(pg.at[: GROUP - 1], pg_s)
-    for b in range(BUCKETS):
-        wait(qc.at[b], s1_s.at[b])
+    wait(like, pa_s)
+    wait(qc, s1_s)
+    for b in range(BUCKETS):
         wait(xr.at[b] if b else fzr, s2_s.at[b])
         wait(zr.at[b] if b else fxr, s3_s.at[b])
         wait(zg.at[b, : NZ - 1] if b else fxg.at[: NX - 1], s4_s.at[b])
@@ -382,9 +379,10 @@
             vmem((b3, n_z, 8, 128), F32),
             vmem((b3, NZ, 8, 128), F32),
             vmem((b3, 2, 4, 8, half), F32),
-            *([dma] * 8),
-            *([dma((b3,))] * 12),
+            *([dma] * 7),
+            *([dma((b3,))] * 10),
             dma((1 + 2 * b3,)),
+            vmem((2 * n_xy + 1 + n_z, PIECE, 128), F32),
             vmem((NZ, RANK, 128), F32),
             vmem((n_z, RANK, 128), F32),
             vmem((NX, 8, 128), F32),

time: 48.8 us -> 48.7 us (level)
  no operation moved by 1% of the time
where the time goes in v7:
time: 48.7 us
  Pallas kernels  48 us (99%)
  between operations  0.64 us (1%)
    pallas_call x1, Pallas kernels, per_device(): pl.pallas_call(reduce_kernel, out_shape=(jax.ShapeDtypeStruct((RANK, widt...  45.7 us
    pallas_call x1, Pallas kernels, per_device(): pl.pallas_call(store_kernel, out_shape=(jax.ShapeDtypeStruct((b3, RANK, w...  2.3 us

profile of v7, /device:TPU:1, one launch (start us, length us, event | category | flops | bytes accessed | tf_op | source)
XLA Modules:
  0.0 48.7 jit_solution(9132098210385720184)
XLA Ops:
  0.6 45.7 %reduce_kernel.1 = (f32[32,1792]{1,0:T(8,128)S(1)}, f32[32,1792]{1,0:T(8,128)S(1)}, f32[32,1792]{1,0:T(8,128)S(1)}, f32[64,1792]{1,0:T(8,128)S(1)}, f32[64,1792]...) custom-call(bf16[1,3,192,1792]{3,2,1,0:T(8,128)(2,1)} %g_hbm.1, ...), custom_call_target="tpu_custom_call" | custom-call | tf_op jit(solution)/shard_map/reduce_kernel/pallas_call | solution.py:354
  46.4 2.3 %store_kernel.1 = (f32[3,32,1792]{2,1,0:T(8,128)}, f32[1,3,192,1792]{3,2,1,0:T(8,128)}) custom-call(f32[32,1792]{1,0:T(8,128)S(1)} %get-tuple-element.14.refs_0_, f32[32,1792]{1,0:T(8,128)S(1)} %get-tuple-element.15.refs_1_, f32[32,1792]{1,0:T(8,128)S(1)} %get-tuple-element.16.refs_2_, f32[64,1792]{1,0:T(8,128)S(1)} %get-tuple-element.17.refs_3_, ...), custom_call_target="tpu_custom_call" | custom-call | tf_op jit(solution)/shard_map/store_kernel/pallas_call | solution.py:398
